TPU v7x, 32 devices: a whole 2x2x4 slice. The times are simulated.
32 devices in a mesh: dp: 8 (over z, y), fsdp: 4 (over x, core).
Axes of the slice: x: 2, y: 2, z: 4, core: 2. Of those that a mesh axis runs over, the one named last changes fastest.
Arguments:
- tokens: bfloat16 [32768, 1024], P(('dp', 'fsdp')), may hold values from -6 to 6
- cotangent: bfloat16 [32768, 1024], P(('dp', 'fsdp')), may hold values from -6 to 6
- lengths: int32 [32, 4], P(('dp', 'fsdp')), may hold values from 0 to 1024, as said below
- attn_gain: bfloat16 [1024], P(('dp', 'fsdp')), may hold values from 0.5 to 1.5
- w_query: bfloat16 [1024, 512], P(('dp', 'fsdp')), may hold values from -0.1875 to 0.1875
- w_key: bfloat16 [1024, 512], P(('dp', 'fsdp')), may hold values from -0.1875 to 0.1875
- w_value: bfloat16 [1024, 1024], P(('dp', 'fsdp')), may hold values from -0.1875 to 0.1875
- w_outgate: bfloat16 [1024, 1024], P(('dp', 'fsdp')), may hold values from -0.1875 to 0.1875
- w_down_rank: bfloat16 [1024, 16], P(('dp', 'fsdp')), may hold values from -0.1875 to 0.1875
- w_up_rank: bfloat16 [16, 512], P(None, ('dp', 'fsdp')), may hold values from -1.5 to 1.5
- rank_bias: bfloat16 [512], P(('dp', 'fsdp')), may hold values from 0.5 to 5
- head_gain: bfloat16 [256], P(('dp', 'fsdp')), may hold values from 0.5 to 1.5
- w_output: bfloat16 [1024, 1024], P(('dp', 'fsdp')), may hold values from -0.375 to 0.375
- ffn_gain: bfloat16 [1024], P(('dp', 'fsdp')), may hold values from 0.5 to 1.5
- w_ffn_gate: bfloat16 [1024, 2816], P(('dp', 'fsdp')), may hold values from -0.1875 to 0.1875
- w_ffn_up: bfloat16 [1024, 2816], P(('dp', 'fsdp')), may hold values from -0.1875 to 0.1875
- w_ffn_down: bfloat16 [2816, 1024], P(('dp', 'fsdp')), may hold values from -0.21875 to 0.21875
Outputs:
- mixed: bfloat16 [32768, 1024], P(('dp', 'fsdp'))
- token_grad: bfloat16 [32768, 1024], P(('dp', 'fsdp'))
- grad_attn_gain: float32 [1024], P(('dp', 'fsdp'))
- grad_query: float32 [1024, 512], P(('dp', 'fsdp'))
- grad_key: float32 [1024, 512], P(('dp', 'fsdp'))
- grad_value: float32 [1024, 1024], P(('dp', 'fsdp'))
- grad_outgate: float32 [1024, 1024], P(('dp', 'fsdp'))
- grad_down_rank: float32 [1024, 16], P(('dp', 'fsdp'))
- grad_up_rank: float32 [16, 512], P(None, ('dp', 'fsdp'))
- grad_rank_bias: float32 [512], P(('dp', 'fsdp'))
- grad_head_gain: float32 [256], P(('dp', 'fsdp'))
- grad_output: float32 [1024, 1024], P(('dp', 'fsdp'))
- grad_ffn_gain: float32 [1024], P(('dp', 'fsdp'))
- grad_ffn_gate: float32 [1024, 2816], P(('dp', 'fsdp'))
- grad_ffn_up: float32 [1024, 2816], P(('dp', 'fsdp'))
- grad_ffn_down: float32 [2816, 1024], P(('dp', 'fsdp'))
Inputs may be any that keep to these rules, and one draw needn't show every extreme that they name: Row i lists the lengths of device i's sequences in slot order; each entry is a multiple of 64, and 0 marks an unused entry. A row sums to between 512 and 1024; slots after the sum are padding. In every draw some device holds a single sequence of 1024 tokens.
All inputs are finite; a program needn't handle non-finite values.
Results may differ from a plain program's by a relative error of at most 0.012.
The roundings to bfloat16 on the way count: a program that leaves them out, or rounds other values in their place, can miss the bound.
Values may be sent and summed in bfloat16 or wider, within the bound.
A program may use at most 256 MiB of HBM per device.

v0:
```python
import jax
import jax.numpy as jnp
from jax import lax
from jax.sharding import PartitionSpec as P

HEADS = 4
DK = 128
DV = 256
GROUP = 64


EPS = 1e-05
HEAD_EPS = 0.1
precise = lax.Precision.HIGHEST


def layout(length_row, slot_count, block_len):
    ends = jnp.cumsum(length_row, dtype=jnp.int32)
    starts = jnp.concatenate([ends - length_row, ends[-1:]])
    begins = jnp.arange(slot_count // block_len, dtype=jnp.int32) * block_len
    restart = jnp.any(begins[:, None] == starts[None, :], axis=1).astype(jnp.float32)
    valid = (jnp.arange(slot_count, dtype=jnp.int32) < ends[-1]).astype(jnp.float32)
    return (restart, valid)


def rms_norm(values, gain, floor_eps=EPS):
    return values * lax.rsqrt(jnp.mean(values * values, axis=-1, keepdims=True) + floor_eps) * gain


def mixer_core(queries, key_rows, val_rows, decay_logit, gate_rows, head_gain, restart):
    blocks = restart.shape[0]
    width = queries.shape[0] // blocks
    decay = jax.nn.log_sigmoid(decay_logit) / 16.0
    scaled = (queries * DK ** (-0.5)).reshape(blocks, width, HEADS, DK)
    keyed = key_rows.reshape(blocks, width, HEADS, DK)
    valued = val_rows.reshape(blocks, width, HEADS, DV)
    cumulative = jnp.cumsum(decay.reshape(blocks, width, HEADS, DK), axis=1)
    block_total = cumulative[:, -1]
    q_read = scaled * jnp.exp(cumulative)
    k_read = keyed * jnp.exp(-cumulative)
    k_write = keyed * jnp.exp(block_total[:, None] - cumulative)
    causal = jnp.tril(jnp.ones((width, width), jnp.float32))
    scores = jnp.einsum("nthc,nshc->nhts", q_read, k_read, precision=precise) * causal
    within = jnp.einsum("nhts,nshv->nthv", scores, valued, precision=precise)
    updates = jnp.einsum("nshc,nshv->nhcv", k_write, valued, precision=precise)

    def advance(carried, inputs_now):
        update_now, total_now, reset_now = inputs_now
        kept = carried * (1.0 - reset_now)
        return (kept * jnp.exp(total_now)[:, :, None] + update_now, kept)

    start_state = jnp.zeros((HEADS, DK, DV), jnp.float32)
    _, before = lax.scan(advance, start_state, (updates, block_total, restart))
    across = jnp.einsum("nthc,nhcv->nthv", q_read, before, precision=precise)
    combined = within + across
    normed = rms_norm(combined, head_gain, HEAD_EPS)
    gates = gate_rows.reshape(blocks, width, HEADS, DV)
    return (normed * jax.nn.silu(gates)).reshape(blocks * width, HEADS * DV)


def swish_product(pre_rows, lin_rows):
    return jax.nn.silu(pre_rows) * lin_rows


def linear(left, right):
    return jnp.dot(left, right, preferred_element_type=jnp.float32)


def linear_tn(left, right):
    return lax.dot_general(
        left, right, (((0,), (0,)), ((), ())), preferred_element_type=jnp.float32
    )


def linear_nt(left, right):
    return lax.dot_general(
        left, right, (((1,), (1,)), ((), ())), preferred_element_type=jnp.float32
    )


def send_ffn(ffn_terms):
    return (
        lax.psum_scatter(ffn_terms[0], ("dp", "fsdp"), scatter_dimension=0, tiled=True),
        lax.psum_scatter(ffn_terms[1], ("dp", "fsdp"), scatter_dimension=0, tiled=True),
        lax.psum_scatter(ffn_terms[2], ("dp", "fsdp"), scatter_dimension=0, tiled=True),
        lax.psum_scatter(ffn_terms[3], ("dp", "fsdp"), scatter_dimension=0, tiled=True),
    )


def local(
    tokens,
    cotangent,
    lengths,
    attn_gain,
    w_query,
    w_key,
    w_value,
    w_outgate,
    w_down_rank,
    w_up_rank,
    rank_bias,
    head_gain,
    w_output,
    ffn_gain,
    w_ffn_gate,
    w_ffn_up,
    w_ffn_down,
):
    mixer = (
        lax.all_gather(attn_gain, ("dp", "fsdp"), axis=0, tiled=True),
        lax.all_gather(w_query, ("dp", "fsdp"), axis=0, tiled=True),
        lax.all_gather(w_key, ("dp", "fsdp"), axis=0, tiled=True),
        lax.all_gather(w_value, ("dp", "fsdp"), axis=0, tiled=True),
        lax.all_gather(w_outgate, ("dp", "fsdp"), axis=0, tiled=True),
        lax.all_gather(w_down_rank, ("dp", "fsdp"), axis=0, tiled=True),
        lax.all_gather(w_up_rank, ("dp", "fsdp"), axis=1, tiled=True),
        lax.all_gather(rank_bias, ("dp", "fsdp"), axis=0, tiled=True),
        lax.all_gather(head_gain, ("dp", "fsdp"), axis=0, tiled=True),
        lax.all_gather(w_output, ("dp", "fsdp"), axis=0, tiled=True),
    )
    ffn = (
        lax.all_gather(ffn_gain, ("dp", "fsdp"), axis=0, tiled=True),
        lax.all_gather(w_ffn_gate, ("dp", "fsdp"), axis=0, tiled=True),
        lax.all_gather(w_ffn_up, ("dp", "fsdp"), axis=0, tiled=True),
        lax.all_gather(w_ffn_down, ("dp", "fsdp"), axis=0, tiled=True),
    )
    (
        full_gain,
        full_query,
        full_key,
        full_value,
        full_outgate,
        full_down_rank,
        full_up_rank,
        full_bias,
        full_head_gain,
        full_output,
    ) = mixer
    ffn_full_gain, full_ffn_gate, full_ffn_up, full_ffn_down = ffn
    restart, valid = layout(lengths[0], tokens.shape[0], GROUP)
    source = tokens.astype(jnp.float32)
    normed_f, norm_in_pull = jax.vjp(rms_norm, source, full_gain.astype(jnp.float32))
    normed_in = normed_f.astype(jnp.bfloat16)
    queries = linear(normed_in, full_query)
    key_rows = linear(normed_in, full_key)
    val_rows = linear(normed_in, full_value)
    gate_rows = linear(normed_in, full_outgate)
    low_rank = linear(normed_in, full_down_rank).astype(jnp.bfloat16)
    decay_logit = linear(low_rank, full_up_rank) + full_bias.astype(jnp.float32)

    def core_of(query_in, key_in, value_in, logit_in, gate_in, gain_in):
        return mixer_core(query_in, key_in, value_in, logit_in, gate_in, gain_in, restart)

    core_out, core_pull = jax.vjp(
        core_of,
        queries,
        key_rows,
        val_rows,
        decay_logit,
        gate_rows,
        full_head_gain.astype(jnp.float32),
    )
    head_out = core_out.astype(jnp.bfloat16)
    middle = source + linear(head_out, full_output)
    normed_mid_f, norm_mid_pull = jax.vjp(rms_norm, middle, ffn_full_gain.astype(jnp.float32))
    normed_mid = normed_mid_f.astype(jnp.bfloat16)
    ffn_pre = linear(normed_mid, full_ffn_gate)
    ffn_lin = linear(normed_mid, full_ffn_up)
    hidden_f, hidden_pull = jax.vjp(swish_product, ffn_pre, ffn_lin)
    hidden = hidden_f.astype(jnp.bfloat16)
    mixed = ((middle + linear(hidden, full_ffn_down)) * valid[:, None]).astype(jnp.bfloat16)
    mixer = (
        lax.all_gather(attn_gain, ("dp", "fsdp"), axis=0, tiled=True),
        lax.all_gather(w_query, ("dp", "fsdp"), axis=0, tiled=True),
        lax.all_gather(w_key, ("dp", "fsdp"), axis=0, tiled=True),
        lax.all_gather(w_value, ("dp", "fsdp"), axis=0, tiled=True),
        lax.all_gather(w_outgate, ("dp", "fsdp"), axis=0, tiled=True),
        lax.all_gather(w_down_rank, ("dp", "fsdp"), axis=0, tiled=True),
        lax.all_gather(w_up_rank, ("dp", "fsdp"), axis=1, tiled=True),
        lax.all_gather(rank_bias, ("dp", "fsdp"), axis=0, tiled=True),
        lax.all_gather(head_gain, ("dp", "fsdp"), axis=0, tiled=True),
        lax.all_gather(w_output, ("dp", "fsdp"), axis=0, tiled=True),
    )
    ffn = (
        lax.all_gather(ffn_gain, ("dp", "fsdp"), axis=0, tiled=True),
        lax.all_gather(w_ffn_gate, ("dp", "fsdp"), axis=0, tiled=True),
        lax.all_gather(w_ffn_up, ("dp", "fsdp"), axis=0, tiled=True),
        lax.all_gather(w_ffn_down, ("dp", "fsdp"), axis=0, tiled=True),
    )
    (
        full_gain,
        full_query,
        full_key,
        full_value,
        full_outgate,
        full_down_rank,
        full_up_rank,
        full_bias,
        full_head_gain,
        full_output,
    ) = mixer
    ffn_full_gain, full_ffn_gate, full_ffn_up, full_ffn_down = ffn
    upstream = cotangent.astype(jnp.float32) * valid[:, None]
    g_out = upstream.astype(jnp.bfloat16)
    grad_ffn_down = linear_tn(hidden, g_out)
    g_hidden = linear_nt(g_out, full_ffn_down)
    g_pre_f, g_lin_f = hidden_pull(g_hidden)
    g_pre = g_pre_f.astype(jnp.bfloat16)
    g_lin = g_lin_f.astype(jnp.bfloat16)
    grad_ffn_gate = linear_tn(normed_mid, g_pre)
    grad_ffn_up = linear_tn(normed_mid, g_lin)
    g_norm_mid = linear_nt(g_pre, full_ffn_gate) + linear_nt(g_lin, full_ffn_up)
    g_mid_norm, grad_ffn_gain = norm_mid_pull(g_norm_mid)
    g_middle = upstream + g_mid_norm
    ffn_terms = (grad_ffn_gain, grad_ffn_gate, grad_ffn_up, grad_ffn_down)
    g_mix = g_middle.astype(jnp.bfloat16)
    grad_output = linear_tn(head_out, g_mix)
    g_head = linear_nt(g_mix, full_output)
    g_queries_f, g_keys_f, g_vals_f, g_logit, g_gates_f, grad_head_gain = core_pull(g_head)
    g_queries = g_queries_f.astype(jnp.bfloat16)
    g_keys = g_keys_f.astype(jnp.bfloat16)
    g_vals = g_vals_f.astype(jnp.bfloat16)
    g_gates = g_gates_f.astype(jnp.bfloat16)
    g_low = g_logit.astype(jnp.bfloat16)
    grad_rank_bias = jnp.sum(g_logit, axis=0)
    grad_up_rank = linear_tn(low_rank, g_low)
    g_rank = linear_nt(g_low, full_up_rank).astype(jnp.bfloat16)
    grad_down_rank = linear_tn(normed_in, g_rank)
    grad_query = linear_tn(normed_in, g_queries)
    grad_key = linear_tn(normed_in, g_keys)
    grad_value = linear_tn(normed_in, g_vals)
    grad_outgate = linear_tn(normed_in, g_gates)
    g_norm_in = (
        linear_nt(g_queries, full_query)
        + linear_nt(g_keys, full_key)
        + linear_nt(g_vals, full_value)
        + linear_nt(g_gates, full_outgate)
        + linear_nt(g_rank, full_down_rank)
    )
    g_source_norm, grad_attn_gain = norm_in_pull(g_norm_in)
    token_grad = (g_middle + g_source_norm).astype(jnp.bfloat16)
    ffn_parts = send_ffn(ffn_terms)
    mixer_parts = (
        lax.psum_scatter(grad_attn_gain, ("dp", "fsdp"), scatter_dimension=0, tiled=True),
        lax.psum_scatter(grad_query, ("dp", "fsdp"), scatter_dimension=0, tiled=True),
        lax.psum_scatter(grad_key, ("dp", "fsdp"), scatter_dimension=0, tiled=True),
        lax.psum_scatter(grad_value, ("dp", "fsdp"), scatter_dimension=0, tiled=True),
        lax.psum_scatter(grad_outgate, ("dp", "fsdp"), scatter_dimension=0, tiled=True),
        lax.psum_scatter(grad_down_rank, ("dp", "fsdp"), scatter_dimension=0, tiled=True),
        lax.psum_scatter(grad_up_rank, ("dp", "fsdp"), scatter_dimension=1, tiled=True),
        lax.psum_scatter(grad_rank_bias, ("dp", "fsdp"), scatter_dimension=0, tiled=True),
        lax.psum_scatter(grad_head_gain, ("dp", "fsdp"), scatter_dimension=0, tiled=True),
        lax.psum_scatter(grad_output, ("dp", "fsdp"), scatter_dimension=0, tiled=True),
    )
    return (
        mixed,
        token_grad,
        mixer_parts[0],
        mixer_parts[1],
        mixer_parts[2],
        mixer_parts[3],
        mixer_parts[4],
        mixer_parts[5],
        mixer_parts[6],
        mixer_parts[7],
        mixer_parts[8],
        mixer_parts[9],
        ffn_parts[0],
        ffn_parts[1],
        ffn_parts[2],
        ffn_parts[3],
    )


def solution(mesh):
    return jax.shard_map(
        local,
        mesh=mesh,
        in_specs=(
            P(("dp", "fsdp"), None),
            P(("dp", "fsdp"), None),
            P(("dp", "fsdp"), None),
            P(("dp", "fsdp")),
            P(("dp", "fsdp"), None),
            P(("dp", "fsdp"), None),
            P(("dp", "fsdp"), None),
            P(("dp", "fsdp"), None),
            P(("dp", "fsdp"), None),
            P(None, ("dp", "fsdp")),
            P(("dp", "fsdp")),
            P(("dp", "fsdp")),
            P(("dp", "fsdp"), None),
            P(("dp", "fsdp")),
            P(("dp", "fsdp"), None),
            P(("dp", "fsdp"), None),
            P(("dp", "fsdp"), None),
        ),
        out_specs=(
            P(("dp", "fsdp"), None),
            P(("dp", "fsdp"), None),
            P(("dp", "fsdp")),
            P(("dp", "fsdp"), None),
            P(("dp", "fsdp"), None),
            P(("dp", "fsdp"), None),
            P(("dp", "fsdp"), None),
            P(("dp", "fsdp"), None),
            P(None, ("dp", "fsdp")),
            P(("dp", "fsdp")),
            P(("dp", "fsdp")),
            P(("dp", "fsdp"), None),
            P(("dp", "fsdp")),
            P(("dp", "fsdp"), None),
            P(("dp", "fsdp"), None),
            P(("dp", "fsdp"), None),
        ),
        check_vma=False,
    )
```

profile of v0, /device:TPU:0, one launch (start us, length us, event | category | flops | bytes accessed | tf_op | source)
XLA Modules:
  0.0 2136.0 jit_solution(8182342519122679118)
XLA Ops:
  19.2 42.3 %all-reduce.10 = (bf16[1024]{0:T(1024)(128)(2,1)S(1)}, bf16[512]{0:T(512)(128)(2,1)S(1)}, bf16[256]{0:T(256)(128)(2,1)S(1)}, bf16[1024]{0:T(1024)(128)(2,1)S(1)}) all-reduce(bf16[1024]{0:T(1024)(128)(2,1)S(1)} %dynamic-update-slice, bf16[512]{0:T(512)(128)(2,1)S(1)} %dynamic-update-slice.1, ...), channel_id=1, replica_groups=mesh['dp'=8,'fsdp'=4] {'dp','fsdp'}, use_global_device_ids=true, to_apply=%add.1 | all-reduce | flops 2816 | bytes 11264
  61.5 40.4 %all-gather = bf16[32,32,16]{1,2,0:T(8,128)(2,1)S(1)} all-gather(bf16[1,32,16]{1,2,0:T(8,128)(2,1)S(1)} %bitcast.221), channel_id=1, replica_groups=mesh['dp'=8,'fsdp'=4] {'dp','fsdp'}, dimensions={0}, use_global_device_ids=true | all-gather | bytes 33792 | tf_op jit(solution)/shard_map/all_gather | solution.py:115
  102.3 37.1 %all_gather.56 = bf16[16,512]{0,1:T(8,128)(2,1)S(1)} all-gather(bf16[16,16]{0,1:T(8,128)(2,1)S(1)} %copy.154), channel_id=1, replica_groups=mesh['dp'=8,'fsdp'=4] {'dp','fsdp'}, dimensions={1}, use_global_device_ids=true | all-gather | bytes 16896 | tf_op jit(solution)/shard_map/all_gather | solution.py:116
  154.2 4.6 fusion.112
  161.8 4.6 convolution_multiply_fusion
  173.1 5.5 fusion.93
  181.6 6.8 fusion.116
  188.4 5.8 reshape.189
  194.2 14.2 fusion.31
  212.8 73.3 %while.38 = (s32[]{:T(128)}, f32[4,128,256]{2,1,0:T(8,128)S(1)}, f32[16,4,128,256]{3,2,1,0:T(8,128)}, f32[16]{0:T(128)S(1)}, f32[16,4,128]{2,1,0:T(4,128)S(1)}, ...) while((s32[]{:T(128)}, f32[4,128,256]{2,1,0:T(8,128)S(1)}, ...), condition=%wide.region_5.6_spmd.clone, body=%wide.region_4.5_spmd.clone.sunk | while | flops 786436 | bytes 2635980 | solution.py:53
  286.1 6.2 fusion.110
  292.3 6.0 reshape.195
  298.3 7.3 fusion.120
  305.6 5.6 fusion.22
  316.8 5.5 multiply_reduce_fusion.3
  326.1 40.4 %all-gather.20.cloned.1.call-done = bf16[1024,2816]{1,0:T(8,128)(2,1)} async-done(((bf16[32,2816]{1,0:T(8,128)(2,1)}), bf16[1024,2816]{1,0:T(8,128)(2,1)}) %all-gather.20.cloned.1.call-update) | async-done | bytes 5767184 | tf_op jit(solution)/shard_map/all_gather | solution.py:123
  366.6 11.8 fusion.121
  378.4 57.3 %all-gather.22.cloned.1.call-done = bf16[1024,2816]{1,0:T(8,128)(2,1)} async-done(((bf16[32,2816]{1,0:T(8,128)(2,1)}), bf16[1024,2816]{1,0:T(8,128)(2,1)}) %all-gather.22.cloned.1.call-update) | async-done | bytes 5767184 | tf_op jit(solution)/shard_map/all_gather | solution.py:124
  435.7 11.9 fusion.122
  447.6 57.2 %all-gather.24.cloned.1.call-done = bf16[2816,1024]{1,0:T(8,128)(2,1)} async-done(((bf16[88,1024]{1,0:T(8,128)(2,1)}), bf16[2816,1024]{1,0:T(8,128)(2,1)}) %all-gather.24.cloned.1.call-update) | async-done | bytes 5767184 | tf_op jit(solution)/shard_map/all_gather | solution.py:125
  504.8 22.0 %multiply_convert_fusion = (bf16[1024,2816]{1,0:T(8,128)(2,1)}, bf16[1024,2816]{1,0:T(8,128)(2,1)}, bf16[1024,2816]{1,0:T(8,128)(2,1)}) fusion(f32[1024,2816]{1,0:T(8,128)} %fusion.121, f32[1024,2816]{1,0:T(8,128)} %fusion.122, bf16[2816,1024]{1,0:T(8,128)(2,1)} %all-gather.24.cloned.1.call-done, bf16[1024,1024]{0,1:T(8,128)(2,1)} %copy.170, ...), kind=kOutput, calls=%fused_computation.21 | convolution fusion | flops 5954863104 | bytes 48238592 | tf_op jit(solution)/shard_map/dot_general | solution.py:76
  526.8 11.4 fusion.123
  538.2 9.4 multiply_reduce_fusion
  555.1 5.6 reshape.196
  560.8 7.9 multiply_reduce_fusion.1
  570.3 9.7 fusion.125
  580.0 5.6 fusion.29
  585.7 10.2 fusion.124
  600.4 79.2 %while.39 = (s32[]{:T(128)}, f32[4,128,256]{2,1,0:T(8,128)S(1)}, f32[16,4,128,256]{3,2,1,0:T(8,128)}, f32[16,4,128]{2,1,0:T(4,128)S(1)}, f32[16,4,128,256]{3,2,1...) while((s32[]{:T(128)}, f32[4,128,256]{2,1,0:T(8,128)S(1)}, ...), condition=%wide.region_12.13_spmd.clone, body=%wide.region_10.12_spmd.clone.sunk | while | flops 917508 | bytes 3160236 | solution.py:53
  679.7 15.4 fusion.72
  698.4 7.2 fusion.47
  730.9 8.3 fusion.94
  751.8 7.2 fusion.81
  769.1 11.8 fusion.128
  781.0 11.9 fusion.129
  793.3 12.0 fusion.62
  819.0 40.1 %all-reduce.9 = (f32[1024]{0:T(1024)S(1)}, f32[512]{0:T(512)S(1)}, f32[256]{0:T(256)S(1)}, f32[1024]{0:T(1024)S(1)}) all-reduce(f32[1024]{0:T(1024)S(1)} %get-tuple-element.416, f32[512]{0:T(512)S(1)} %neg.54, f32[256]{0:T(256)S(1)} %get-tuple-element.414, f32[1024]{0:T(1024)S(1)} %copy-done.53), channel_id=2, replica_groups=mesh['dp'=8,'fsdp'=4] {'dp','fsdp'}, use_global_device_ids=true, to_apply=%region_17.18.clone | all-reduce | flops 2816 | bytes 22528
  860.3 5.8 fusion.19
  870.1 10.6 multiply_convert_fusion.2
  885.8 92.3 %reduce-scatter.31.cloned.1.call-done = f32[32,16]{1,0:T(8,128)} async-done(((f32[1024,16]{1,0:T(8,128)}), f32[32,16]{1,0:T(8,128)}) %reduce-scatter.31.cloned.1.call-update) | async-done | bytes 2064
  979.5 134.1 %reduce-scatter.15.cloned.1.call-done = f32[32,512]{1,0:T(8,128)} async-done(((f32[1024,512]{1,0:T(8,128)}), f32[32,512]{1,0:T(8,128)}) %reduce-scatter.15.cloned.1.call-update) | async-done | bytes 65552 | tf_op jit(solution)/shard_map/reduce_scatter | solution.py:245
  1113.5 135.3 %reduce-scatter.17.cloned.1.call-done = f32[32,512]{1,0:T(8,128)} async-done(((f32[1024,512]{1,0:T(8,128)}), f32[32,512]{1,0:T(8,128)}) %reduce-scatter.17.cloned.1.call-update) | async-done | bytes 65552 | tf_op jit(solution)/shard_map/reduce_scatter | solution.py:246
  1248.8 139.9 %reduce-scatter.19.cloned.1.call-done = f32[32,1024]{1,0:T(8,128)} async-done(((f32[1024,1024]{1,0:T(8,128)}), f32[32,1024]{1,0:T(8,128)}) %reduce-scatter.19.cloned.1.call-update) | async-done | bytes 131088 | tf_op jit(solution)/shard_map/reduce_scatter | solution.py:247
  1388.7 139.8 %reduce-scatter.23.cloned.1.call-done = f32[32,1024]{1,0:T(8,128)} async-done(((f32[1024,1024]{1,0:T(8,128)}), f32[32,1024]{1,0:T(8,128)}) %reduce-scatter.23.cloned.1.call-update) | async-done | bytes 131088 | tf_op jit(solution)/shard_map/reduce_scatter | solution.py:253
  1528.5 139.9 %reduce-scatter.21.cloned.1.call-done = f32[32,1024]{1,0:T(8,128)} async-done(((f32[1024,1024]{1,0:T(8,128)}), f32[32,1024]{1,0:T(8,128)}) %reduce-scatter.21.cloned.1.call-update) | async-done | bytes 131088 | tf_op jit(solution)/shard_map/reduce_scatter | solution.py:248
  1668.4 153.6 %reduce-scatter.25.cloned.1.call-done = f32[32,2816]{1,0:T(8,128)} async-done(((f32[1024,2816]{1,0:T(8,128)}), f32[32,2816]{1,0:T(8,128)}) %reduce-scatter.25.cloned.1.call-update) | async-done | bytes 360464 | tf_op jit(solution)/shard_map/reduce_scatter | solution.py:84
  1822.0 153.5 %reduce-scatter.27.cloned.1.call-done = f32[32,2816]{1,0:T(8,128)} async-done(((f32[1024,2816]{1,0:T(8,128)}), f32[32,2816]{1,0:T(8,128)}) %reduce-scatter.27.cloned.1.call-update) | async-done | bytes 360464 | tf_op jit(solution)/shard_map/reduce_scatter | solution.py:85
  1975.5 153.5 %reduce-scatter.29.cloned.1.call-done = f32[88,1024]{1,0:T(8,128)} async-done(((f32[2816,1024]{1,0:T(8,128)}), f32[88,1024]{1,0:T(8,128)}) %reduce-scatter.29.cloned.1.call-update) | async-done | bytes 360464 | tf_op jit(solution)/shard_map/reduce_scatter | solution.py:86
  (427 shorter events, 295.9 us)
Async XLA Ops:
  7.2 11.1 copy-start.58
  7.2 11.3 copy-start.59
  7.2 11.5 copy-start.60
  7.2 11.8 copy-start.61
  7.2 54.3 %copy-start.51 = (bf16[32,16]{0,1:T(8,128)(2,1)S(1)}, bf16[32,16]{0,1:T(8,128)(2,1)}, u32[]{:S(2)}) copy-start(bf16[32,16]{0,1:T(8,128)(2,1)} %param.29) | copy-start | bytes 3076
  7.2 94.9 %copy-start.52 = (bf16[16,16]{1,0:T(8,128)(2,1)S(1)}, bf16[16,16]{1,0:T(8,128)(2,1)}, u32[]{:S(2)}) copy-start(bf16[16,16]{1,0:T(8,128)(2,1)} %param.30) | copy-start | bytes 1540
  7.2 146.9 %all-gather.14.cloned.1.call-start = ((), (), s32[]{:S(2)}) async-start(), calls=%async_computation.12 | async-start | bytes 1081344 | tf_op jit(solution)/shard_map/all_gather | solution.py:112
  8.0 153.8 %all-gather.12.cloned.1.call-start = ((), (), s32[]{:S(2)}) async-start(), calls=%async_computation.11 | async-start | bytes 1081344 | tf_op jit(solution)/shard_map/all_gather | solution.py:111
  8.7 172.9 %all-gather.10.cloned.1.call-start = ((), (), s32[]{:S(2)}) async-start(), calls=%async_computation.10 | async-start | bytes 2162688 | tf_op jit(solution)/shard_map/all_gather | solution.py:113
  9.5 276.6 %all-gather.16.cloned.1.call-start = ((), (), s32[]{:S(2)}) async-start(), calls=%async_computation.13 | async-start | bytes 2162688 | tf_op jit(solution)/shard_map/all_gather | solution.py:114
  10.0 306.8 %all-gather.18.cloned.1.call-start = ((), (), s32[]{:S(2)}) async-start(), calls=%async_computation.14 | async-start | bytes 2162688 | tf_op jit(solution)/shard_map/all_gather | solution.py:119
  10.6 355.9 %all-gather.20.cloned.1.call-start = ((), (), s32[]{:S(2)}) async-start(), calls=%async_computation.15 | async-start | bytes 5947392 | tf_op jit(solution)/shard_map/all_gather | solution.py:123
  11.2 424.5 %all-gather.22.cloned.1.call-start = ((), (), s32[]{:S(2)}) async-start(), calls=%async_computation.16 | async-start | bytes 5947392 | tf_op jit(solution)/shard_map/all_gather | solution.py:124
  11.9 492.8 %all-gather.24.cloned.1.call-start = ((), (), s32[]{:S(2)}) async-start(), calls=%async_computation.17 | async-start | bytes 5947392 | tf_op jit(solution)/shard_map/all_gather | solution.py:125
  12.7 871.7 %reduce-scatter.33.cloned.1.call-start = ((), (), s32[]{:S(2)}) async-start(), calls=%async_computation.27 | async-start | bytes 270336
  17.7 125.7 %copy-start.15 = (bf16[1024,1024]{0,1:T(8,128)(2,1)}, bf16[1024,1024]{0,1:T(8,128)(2,1)S(1)}, u32[]{:S(2)}) copy-start(bf16[1024,1024]{0,1:T(8,128)(2,1)S(1)} %copy.152) | copy-start | bytes 6291460
  18.2 43.3 %copy-start.45 = (f32[1024]{0:T(1024)}, f32[1024]{0:T(1024)S(1)}, u32[]{:S(2)}) copy-start(f32[1024]{0:T(1024)S(1)} %fusion.20) | copy-start | bytes 12292
  18.2 267.8 %copy-start.41 = (f32[1024]{0:T(1024)}, f32[1024]{0:T(1024)S(1)}, u32[]{:S(2)}) copy-start(f32[1024]{0:T(1024)S(1)} %fusion.98) | copy-start | bytes 12292
  61.5 224.6 %copy-start.43 = (f32[1024]{0:T(1024)}, f32[1024]{0:T(1024)S(1)}, u32[]{:S(2)}) copy-start(f32[1024]{0:T(1024)S(1)} %convert_element_type.98) | copy-start | bytes 12292
  102.1 41.2 %copy-start.38 = (bf16[1024,16]{0,1:T(8,128)(2,1)}, bf16[1024,16]{0,1:T(8,128)(2,1)S(1)}, u32[]{:S(2)}) copy-start(bf16[1024,16]{0,1:T(8,128)(2,1)S(1)} %reshape.206) | copy-start | bytes 98308
  102.2 41.2 %copy-start.49 = (f32[512]{0:T(512)}, f32[512]{0:T(512)S(1)}, u32[]{:S(2)}) copy-start(f32[512]{0:T(512)S(1)} %convert_element_type.101) | copy-start | bytes 6148
  148.6 45.6 %copy-start = (f32[16,64,4,128]{3,0,1,2:T(8,128)}, f32[16,64,4,128]{3,0,1,2:T(8,128)S(1)}, u32[]{:S(2)}) copy-start(f32[16,64,4,128]{3,0,1,2:T(8,128)S(1)} %fusion.54) | copy-start | bytes 6291460
  212.8 73.3 %copy-start.16 = (bf16[1024,1024]{0,1:T(8,128)(2,1)S(1)}, bf16[1024,1024]{0,1:T(8,128)(2,1)}, u32[]{:S(2)}) copy-start(bf16[1024,1024]{0,1:T(8,128)(2,1)} %copy-done.15) | copy-start | bytes 6291460
  526.8 11.4 copy-start.24
  526.8 11.4 copy-start.54
  526.8 11.4 copy-start.64
  538.2 9.5 copy-start.26
  568.8 16.9 slice-start
  570.3 15.3 copy-start.2
  570.3 9.7 copy-start.5
  570.3 15.3 slice-start.1
  600.4 79.3 %copy-start.1 = (f32[16,64,4,128]{3,0,1,2:T(8,128)S(1)}, f32[16,64,4,128]{3,0,1,2:T(8,128)}, u32[]{:S(2)}) copy-start(f32[16,64,4,128]{3,0,1,2:T(8,128)} %copy-done) | copy-start | bytes 6291460
  600.4 79.3 %copy-start.35 = (f32[16,4,128]{2,1,0:T(4,128)S(1)}, f32[16,4,128]{2,1,0:T(4,128)}, u32[]{:S(2)}) copy-start(f32[16,4,128]{2,1,0:T(4,128)} %copy-done.34) | copy-start | bytes 98308
  679.7 15.5 copy-start.7
  679.7 15.5 copy-start.18
  679.7 15.5 copy-start.25
  713.6 264.5 %reduce-scatter.31.cloned.1.call-start = ((), (), s32[]{:S(2)}) async-start(), calls=%async_computation.26 | async-start | bytes 540672
  719.0 394.5 %reduce-scatter.15.cloned.1.call-start = ((), (), s32[]{:S(2)}) async-start(), calls=%async_computation.18 | async-start | bytes 2162688 | tf_op jit(solution)/shard_map/reduce_scatter | solution.py:245
  723.5 525.4 %reduce-scatter.17.cloned.1.call-start = ((), (), s32[]{:S(2)}) async-start(), calls=%async_computation.19 | async-start | bytes 2162688 | tf_op jit(solution)/shard_map/reduce_scatter | solution.py:246
  730.9 657.9 %reduce-scatter.19.cloned.1.call-start = ((), (), s32[]{:S(2)}) async-start(), calls=%async_computation.20 | async-start | bytes 4325376 | tf_op jit(solution)/shard_map/reduce_scatter | solution.py:247
  730.9 8.4 copy-start.3
  730.9 8.4 copy-start.21
  751.8 776.7 %reduce-scatter.23.cloned.1.call-start = ((), (), s32[]{:S(2)}) async-start(), calls=%async_computation.22 | async-start | bytes 4325376 | tf_op jit(solution)/shard_map/reduce_scatter | solution.py:253
  759.1 909.4 %reduce-scatter.21.cloned.1.call-start = ((), (), s32[]{:S(2)}) async-start(), calls=%async_computation.21 | async-start | bytes 4325376 | tf_op jit(solution)/shard_map/reduce_scatter | solution.py:248
  769.1 1052.9 %reduce-scatter.25.cloned.1.call-start = ((), (), s32[]{:S(2)}) async-start(), calls=%async_computation.23 | async-start | bytes 11894784 | tf_op jit(solution)/shard_map/reduce_scatter | solution.py:84
  780.9 1194.6 %reduce-scatter.27.cloned.1.call-start = ((), (), s32[]{:S(2)}) async-start(), calls=%async_computation.24 | async-start | bytes 11894784 | tf_op jit(solution)/shard_map/reduce_scatter | solution.py:85
  792.9 1336.1 %reduce-scatter.29.cloned.1.call-start = ((), (), s32[]{:S(2)}) async-start(), calls=%async_computation.25 | async-start | bytes 11894784 | tf_op jit(solution)/shard_map/reduce_scatter | solution.py:86
  815.3 45.0 %copy-start.46 = (f32[1024]{0:T(1024)S(1)}, f32[1024]{0:T(1024)}, u32[]{:S(2)}) copy-start(f32[1024]{0:T(1024)} %copy-done.45) | copy-start | bytes 12292
  (37 other events, 138.7 us)
Sparse Core Ops, SparseCore 0:
  10.9 56.5 all-gather.13
  70.4 52.9 all-gather.11
  126.3 55.2 all-gather.9
  184.3 55.2 all-gather.15
  242.3 55.3 all-gather.17
  300.4 66.1 all-gather.19
  369.4 66.2 all-gather.21
  438.5 66.2 all-gather.23
  713.7 132.4 reduce-scatter.32
  848.4 129.6 reduce-scatter.30
  980.9 132.5 reduce-scatter.14
  1116.3 132.5 reduce-scatter.16
  1251.7 136.9 reduce-scatter.18
  1391.4 137.0 reduce-scatter.22
  1531.2 137.1 reduce-scatter.20
  1671.2 150.7 reduce-scatter.24
  1824.7 150.7 reduce-scatter.26
  1978.2 150.7 reduce-scatter.28
where the time goes:
time: 2140 us
  waiting for transfers between devices  1400 us (65%)
  matrix products  288 us (13%)
  blocking collectives  160 us (7%)
  other arithmetic  155 us (7%)
  local copies, waits for them, and re-layouts  111 us (5%)
    reduce_scatter x1, waiting for transfers between devices, send_ffn(): lax.psum_scatter(ffn_terms[1], ('dp', 'fsdp'), scatter_dimension=0, tiled...  154 us
    reduce_scatter x1, waiting for transfers between devices, send_ffn(): lax.psum_scatter(ffn_terms[3], ('dp', 'fsdp'), scatter_dimension=0, tiled...  154 us
    reduce_scatter x1, waiting for transfers between devices, send_ffn(): lax.psum_scatter(ffn_terms[2], ('dp', 'fsdp'), scatter_dimension=0, tiled...  153 us
    reduce_scatter x1, waiting for transfers between devices, local(): lax.psum_scatter(grad_outgate, ('dp', 'fsdp'), scatter_dimension=0, tiled...  140 us
    reduce_scatter x1, waiting for transfers between devices, local(): lax.psum_scatter(grad_value, ('dp', 'fsdp'), scatter_dimension=0, tiled=T...  140 us
    reduce_scatter x1, waiting for transfers between devices, local(): lax.psum_scatter(grad_output, ('dp', 'fsdp'), scatter_dimension=0, tiled=...  140 us
    reduce_scatter x1, waiting for transfers between devices, local(): lax.psum_scatter(grad_key, ('dp', 'fsdp'), scatter_dimension=0, tiled=True)  135 us
    reduce_scatter x1, waiting for transfers between devices, local(): lax.psum_scatter(grad_query, ('dp', 'fsdp'), scatter_dimension=0, tiled=T...  134 us
  transfers between devices with their start and end apart: 18, of which 13 were waited for; matrix products, arithmetic and copies ran while one was open for 16% of the time, Pallas kernels for 0%

commit v1 on v0

v1 whole, which is shorter than its diff:
```python
import jax
import jax.numpy as jnp
from jax import lax
from jax.sharding import PartitionSpec as P

HEADS = 4
DK = 128
DV = 256
GROUP = 64


EPS = 1e-05
HEAD_EPS = 0.1
precise = lax.Precision.HIGH


def layout(length_row, slot_count, block_len):
    ends = jnp.cumsum(length_row, dtype=jnp.int32)
    starts = jnp.concatenate([ends - length_row, ends[-1:]])
    begins = jnp.arange(slot_count // block_len, dtype=jnp.int32) * block_len
    restart = jnp.any(begins[:, None] == starts[None, :], axis=1).astype(jnp.float32)
    valid = (jnp.arange(slot_count, dtype=jnp.int32) < ends[-1]).astype(jnp.float32)
    return (restart, valid)


def rms_norm(values, gain, floor_eps=EPS):
    return values * lax.rsqrt(jnp.mean(values * values, axis=-1, keepdims=True) + floor_eps) * gain


def mixer_core(queries, key_rows, val_rows, decay_logit, gate_rows, head_gain, restart):
    blocks = restart.shape[0]
    width = queries.shape[0] // blocks
    decay = jax.nn.log_sigmoid(decay_logit) / 16.0
    scaled = (queries * DK ** (-0.5)).reshape(blocks, width, HEADS, DK)
    keyed = key_rows.reshape(blocks, width, HEADS, DK)
    valued = val_rows.reshape(blocks, width, HEADS, DV)
    cumulative = jnp.cumsum(decay.reshape(blocks, width, HEADS, DK), axis=1)
    block_total = cumulative[:, -1]
    q_read = scaled * jnp.exp(cumulative)
    k_read = keyed * jnp.exp(-cumulative)
    k_write = keyed * jnp.exp(block_total[:, None] - cumulative)
    causal = jnp.tril(jnp.ones((width, width), jnp.float32))
    scores = jnp.einsum("nthc,nshc->nhts", q_read, k_read, precision=precise) * causal
    within = jnp.einsum("nhts,nshv->nthv", scores, valued, precision=precise)
    updates = jnp.einsum("nshc,nshv->nhcv", k_write, valued, precision=precise)

    def advance(carried, inputs_now):
        update_now, total_now, reset_now = inputs_now
        kept = carried * (1.0 - reset_now)
        return (kept * jnp.exp(total_now)[:, :, None] + update_now, kept)

    start_state = jnp.zeros((HEADS, DK, DV), jnp.float32)
    _, before = lax.scan(advance, start_state, (updates, block_total, restart), unroll=True)
    across = jnp.einsum("nthc,nhcv->nthv", q_read, before, precision=precise)
    combined = within + across
    normed = rms_norm(combined, head_gain, HEAD_EPS)
    gates = gate_rows.reshape(blocks, width, HEADS, DV)
    return (normed * jax.nn.silu(gates)).reshape(blocks * width, HEADS * DV)


def swish_product(pre_rows, lin_rows):
    return jax.nn.silu(pre_rows) * lin_rows


def linear(left, right):
    return jnp.dot(left, right, preferred_element_type=jnp.float32)


def linear_tn(left, right):
    return lax.dot_general(
        left, right, (((0,), (0,)), ((), ())), preferred_element_type=jnp.float32
    )


def linear_nt(left, right):
    return lax.dot_general(
        left, right, (((1,), (1,)), ((), ())), preferred_element_type=jnp.float32
    )


AXES = ("dp", "fsdp")
SMALL = 128


def gather(shard):
    return lax.all_gather(shard, AXES, axis=0, tiled=True)


def scatter(term):
    return lax.psum_scatter(term, AXES, scatter_dimension=0, tiled=True)


def pack_small(parts, rows):
    flat = jnp.concatenate(parts, axis=1)
    owners, width = flat.shape
    flat = jnp.pad(flat, ((0, 0), (0, rows * SMALL - width)))
    return flat.reshape(owners * rows, SMALL)


def unpack_small(block, owners, widths):
    flat = block.reshape(owners, -1)
    parts, at = [], 0
    for width in widths:
        parts.append(flat[:, at : at + width])
        at += width
    return parts


def local(
    tokens,
    cotangent,
    lengths,
    attn_gain,
    w_query,
    w_key,
    w_value,
    w_outgate,
    w_down_rank,
    w_up_rank,
    rank_bias,
    head_gain,
    w_output,
    ffn_gain,
    w_ffn_gate,
    w_ffn_up,
    w_ffn_down,
):
    rows, keys = w_query.shape
    model = tokens.shape[1]
    owners = model // rows
    vals = w_value.shape[1]
    rank = w_down_rank.shape[1]
    inner = w_ffn_gate.shape[1]
    wide = 2 * keys + 2 * vals
    shards = (w_down_rank, attn_gain, w_up_rank, rank_bias, head_gain, ffn_gain)
    widths = [shard.size for shard in shards]
    small_shard = jnp.concatenate([shard.reshape(-1) for shard in shards])
    small_shard = jnp.pad(small_shard, (0, rows * SMALL - sum(widths))).reshape(rows, SMALL)
    mixer = gather(
        jnp.concatenate([w_query, w_key, w_value, w_outgate, w_output, small_shard], axis=1)
    )
    full_gate_up = gather(jnp.concatenate([w_ffn_gate, w_ffn_up], axis=1))
    full_ffn_down = gather(w_ffn_down)
    full_in = mixer[:, :wide]
    full_output = mixer[:, wide : wide + model]
    small = unpack_small(mixer[:, wide + model :], owners, widths)
    full_down_rank = small[0].reshape(model, rank)
    full_gain = small[1].reshape(-1)
    full_up_rank = small[2].reshape(owners, rank, -1).transpose(1, 0, 2).reshape(rank, keys)
    full_bias = small[3].reshape(-1)
    full_head_gain = small[4].reshape(-1)
    ffn_full_gain = small[5].reshape(-1)
    restart, valid = layout(lengths[0], tokens.shape[0], GROUP)
    source = tokens.astype(jnp.float32)
    normed_f, norm_in_pull = jax.vjp(rms_norm, source, full_gain.astype(jnp.float32))
    normed_in = normed_f.astype(jnp.bfloat16)
    projected = linear(normed_in, full_in)
    queries = projected[:, :keys]
    key_rows = projected[:, keys : 2 * keys]
    val_rows = projected[:, 2 * keys : 2 * keys + vals]
    gate_rows = projected[:, 2 * keys + vals :]
    low_rank = linear(normed_in, full_down_rank).astype(jnp.bfloat16)
    decay_logit = linear(low_rank, full_up_rank) + full_bias.astype(jnp.float32)

    def core_of(query_in, key_in, value_in, logit_in, gate_in, gain_in):
        return mixer_core(query_in, key_in, value_in, logit_in, gate_in, gain_in, restart)

    core_out, core_pull = jax.vjp(
        core_of,
        queries,
        key_rows,
        val_rows,
        decay_logit,
        gate_rows,
        full_head_gain.astype(jnp.float32),
    )
    head_out = core_out.astype(jnp.bfloat16)
    middle = source + linear(head_out, full_output)
    normed_mid_f, norm_mid_pull = jax.vjp(rms_norm, middle, ffn_full_gain.astype(jnp.float32))
    normed_mid = normed_mid_f.astype(jnp.bfloat16)
    ffn_both = linear(normed_mid, full_gate_up)
    ffn_pre = ffn_both[:, :inner]
    ffn_lin = ffn_both[:, inner:]
    hidden_f, hidden_pull = jax.vjp(swish_product, ffn_pre, ffn_lin)
    hidden = hidden_f.astype(jnp.bfloat16)
    mixed = ((middle + linear(hidden, full_ffn_down)) * valid[:, None]).astype(jnp.bfloat16)
    upstream = cotangent.astype(jnp.float32) * valid[:, None]
    g_out = upstream.astype(jnp.bfloat16)
    grad_ffn_down = linear_tn(hidden, g_out)
    g_hidden = linear_nt(g_out, full_ffn_down)
    g_pre_f, g_lin_f = hidden_pull(g_hidden)
    g_both = jnp.concatenate([g_pre_f, g_lin_f], axis=1).astype(jnp.bfloat16)
    grad_gate_up = linear_tn(normed_mid, g_both)
    g_norm_mid = linear_nt(g_both, full_gate_up)
    g_mid_norm, grad_ffn_gain = norm_mid_pull(g_norm_mid)
    g_middle = upstream + g_mid_norm
    g_mix = g_middle.astype(jnp.bfloat16)
    grad_output = linear_tn(head_out, g_mix)
    g_mix, grad_ffn_down, grad_gate_up = lax.optimization_barrier(
        (g_mix, grad_ffn_down, grad_gate_up)
    )
    down_part = scatter(grad_ffn_down)
    gate_up_part = scatter(grad_gate_up)
    g_head = linear_nt(g_mix, full_output)
    g_queries_f, g_keys_f, g_vals_f, g_logit, g_gates_f, grad_head_gain = core_pull(g_head)
    g_in = jnp.concatenate([g_queries_f, g_keys_f, g_vals_f, g_gates_f], axis=1).astype(
        jnp.bfloat16
    )
    g_low = g_logit.astype(jnp.bfloat16)
    grad_rank_bias = jnp.sum(g_logit, axis=0)
    grad_up_rank = linear_tn(low_rank, g_low)
    g_rank = linear_nt(g_low, full_up_rank).astype(jnp.bfloat16)
    grad_down_rank = linear_tn(normed_in, g_rank)
    grad_in = linear_tn(normed_in, g_in)
    g_norm_in = linear_nt(g_in, full_in) + linear_nt(g_rank, full_down_rank)
    g_source_norm, grad_attn_gain = norm_in_pull(g_norm_in)
    token_grad = (g_middle + g_source_norm).astype(jnp.bfloat16)
    terms = (
        grad_down_rank,
        grad_attn_gain,
        grad_up_rank.reshape(rank, owners, -1).transpose(1, 0, 2),
        grad_rank_bias,
        grad_head_gain,
        grad_ffn_gain,
    )
    small_terms = pack_small([term.reshape(owners, -1) for term in terms], rows)
    part = scatter(jnp.concatenate([grad_in, grad_output, small_terms], axis=1))
    small_part = unpack_small(part[:, wide + model :], 1, widths)
    return (
        mixed,
        token_grad,
        small_part[1].reshape(-1),
        part[:, :keys],
        part[:, keys : 2 * keys],
        part[:, 2 * keys : 2 * keys + vals],
        part[:, 2 * keys + vals : wide],
        small_part[0].reshape(rows, rank),
        small_part[2].reshape(rank, -1),
        small_part[3].reshape(-1),
        small_part[4].reshape(-1),
        part[:, wide : wide + model],
        small_part[5].reshape(-1),
        gate_up_part[:, :inner],
        gate_up_part[:, inner:],
        down_part,
    )


def solution(mesh):
    return jax.shard_map(
        local,
        mesh=mesh,
        in_specs=(
            P(("dp", "fsdp"), None),
            P(("dp", "fsdp"), None),
            P(("dp", "fsdp"), None),
            P(("dp", "fsdp")),
            P(("dp", "fsdp"), None),
            P(("dp", "fsdp"), None),
            P(("dp", "fsdp"), None),
            P(("dp", "fsdp"), None),
            P(("dp", "fsdp"), None),
            P(None, ("dp", "fsdp")),
            P(("dp", "fsdp")),
            P(("dp", "fsdp")),
            P(("dp", "fsdp"), None),
            P(("dp", "fsdp")),
            P(("dp", "fsdp"), None),
            P(("dp", "fsdp"), None),
            P(("dp", "fsdp"), None),
        ),
        out_specs=(
            P(("dp", "fsdp"), None),
            P(("dp", "fsdp"), None),
            P(("dp", "fsdp")),
            P(("dp", "fsdp"), None),
            P(("dp", "fsdp"), None),
            P(("dp", "fsdp"), None),
            P(("dp", "fsdp"), None),
            P(("dp", "fsdp"), None),
            P(None, ("dp", "fsdp")),
            P(("dp", "fsdp")),
            P(("dp", "fsdp")),
            P(("dp", "fsdp"), None),
            P(("dp", "fsdp")),
            P(("dp", "fsdp"), None),
            P(("dp", "fsdp"), None),
            P(("dp", "fsdp"), None),
        ),
        check_vma=False,
    )
```

time: 2140 us -> 1120 us (0.52)
  waiting for transfers between devices: 1400 us -> 664 us
  blocking collectives: 160 us -> 0 us
  matrix products: 288 us -> 229 us
  other arithmetic: 155 us -> 101 us
    reduce_scatter x8 -> x3, waiting for transfers between devices: 1150 us -> 565 us  [scatter(): return lax.psum_scatter(term, AXES, scatter_dimension=0, tiled=True)]
    unnamed x20 -> x6, waiting for transfers between devices: 97.5 us -> 1.79 us
    unnamed x2 -> x0, blocking collectives: 82.4 us -> none
    all_gather x2 -> x0, blocking collectives: 77.5 us -> none  [the longest x1 40.4 us: local(): lax.all_gather(w_down_rank, ('dp', 'fsdp'), axis=0, tiled=True)]
    all_gather x8 -> x3, waiting for transfers between devices: 158 us -> 97.7 us  [gather(): return lax.all_gather(shard, AXES, axis=0, tiled=True)]
    dynamic_update_slice x64 -> x0, other arithmetic: 58.2 us -> none  [mixer_core(): _, before = lax.scan(advance, start_state, (updates, block_total, restart))]
    unnamed x3 -> x42, other arithmetic: 0.01 us -> 34.9 us
    add x17 -> x0, other arithmetic: 31.1 us -> none  [the longest x16 30 us: advance(): return (kept * jnp.exp(total_now)[:, :, None] + update_now, kept)]
  transfers between devices with their start and end apart: 18 -> 6, of which waited for: 13 -> 5; matrix products, arithmetic and copies ran while one was open for 16% -> 15% of each run, Pallas kernels for 0% -> 0%
where the time goes in v1:
time: 1120 us; the launch traced here: 1110 us
  waiting for transfers between devices  664 us (59%)
  matrix products  229 us (20%)
  other arithmetic  101 us (9%)
  local copies, waits for them, and re-layouts  92.7 us (8%)
  between operations  26.5 us (2%)
    reduce_scatter x3, waiting for transfers between devices, scatter(): return lax.psum_scatter(term, AXES, scatter_dimension=0, tiled=True)  565 us
    all_gather x3, waiting for transfers between devices, gather(): return lax.all_gather(shard, AXES, axis=0, tiled=True)  97.7 us
    dot_general x6, matrix products, linear_nt(): lax.dot_general(left, right, (((1,), (1,)), ((), ())), preferred_element_...  57.4 us
    dot_general x6, matrix products, linear(): return jnp.dot(left, right, preferred_element_type=jnp.float32)  53.2 us
    dot_general x6, matrix products, linear_tn(): lax.dot_general(left, right, (((0,), (0,)), ((), ())), preferred_element_...  48.8 us
    unnamed x235, local copies, waits for them, and re-layouts  35.6 us
    unnamed x42, other arithmetic  34.9 us
    dot_general x3, matrix products, mixer_core(): updates = jnp.einsum('nshc,nshv->nhcv', k_write, valued, precision=precise)  28.9 us
  transfers between devices with their start and end apart: 6, of which 5 were waited for; matrix products, arithmetic and copies ran while one was open for 15% of the time, Pallas kernels for 0%

profile of v1, /device:TPU:0, one launch (start us, length us, event | category | flops | bytes accessed | tf_op | source)
XLA Modules:
  0.0 1113.3 jit_solution(6674382766877707615)
XLA Ops:
  12.9 2.8 concatenate.42
  24.2 2.9 copy.208
  37.8 4.0 copy.241
  41.8 55.9 %all-gather.4.cloned.1.call-done = bf16[1024,4224]{1,0:T(8,128)(2,1)} async-done(((bf16[32,4224]{1,0:T(8,128)(2,1)}), bf16[1024,4224]{1,0:T(8,128)(2,1)}) %all-gather.4.cloned.1.call-update) | async-done | bytes 8650768 | tf_op jit(solution)/shard_map/all_gather | solution.py:86
  99.0 9.3 fusion.8
  108.3 4.1 fusion.167
  112.4 2.5 slice_multiply_fusion
  116.5 2.7 negate_multiply_fusion
  124.7 5.7 reshape.771
  130.4 2.9 reshape.777
  133.3 2.9 reshape.772
  136.3 5.8 reshape.780
  142.1 7.6 fusion.32
  149.7 2.4 broadcast_multiply_fusion
  167.0 3.1 fusion.81
  170.4 5.0 fusion.148
  175.4 5.8 fusion.23
  187.0 7.1 multiply_reduce_fusion.3
  196.5 21.3 %fusion.141 = f32[1024,5632]{1,0:T(8,128)} fusion(bf16[1024,5632]{1,0:T(8,128)(2,1)} %all-gather.6.cloned.1.call-done, f32[1024,1024]{0,1:T(8,128)} %get-tuple-element.204, f32[1024]{0:T(1024)S(1)} %reshape.802, f32[1024]{0:T(1024)S(1)} %fusion.136), kind=kOutput, calls=%fused_computation.341 | convolution fusion | flops 11814305792 | bytes 38805504 | tf_op jit(solution)/shard_map/dot_general | solution.py:66
  217.8 41.8 %all-gather.8.cloned.1.call-done = bf16[2816,1024]{1,0:T(8,128)(2,1)} async-done(((bf16[88,1024]{1,0:T(8,128)(2,1)}), bf16[2816,1024]{1,0:T(8,128)(2,1)}) %all-gather.8.cloned.1.call-update) | async-done | bytes 5767184 | tf_op jit(solution)/shard_map/all_gather | solution.py:86
  259.6 20.2 %fusion.2 = (bf16[1024,2816]{1,0:T(8,128)(2,1)}, bf16[1024,2816]{1,0:T(8,128)(2,1)}, bf16[1024,2816]{1,0:T(8,128)(2,1)}) fusion(f32[1024,5632]{1,0:T(8,128)} %fusion.141, bf16[2816,1024]{1,0:T(8,128)(2,1)} %all-gather.8.cloned.1.call-done, bf16[1024,1024]{0,1:T(8,128)(2,1)S(1)} %copy-done.21, f32[1024]{0:T(1024)S(1)} %fusion.134), kind=kOutput, calls=%fused_computation.4 | convolution fusion | flops 5954863104 | bytes 48238592 | tf_op jit(solution)/shard_map/dot_general | solution.py:76
  279.8 21.9 %fusion.4 = f32[1024,5632]{1,0:T(8,128)} fusion(bf16[1024,2816]{1,0:T(8,128)(2,1)} %get-tuple-element.146, bf16[1024,2816]{1,0:T(8,128)(2,1)} %get-tuple-element.145, f32[1024,1024]{0,1:T(8,128)} %get-tuple-element.204, f32[1024]{0:T(1024)S(1)} %reshape.802, f32[1024]{0:T(1024)S(1)} %fusion.136), kind=kOutput, calls=%fused_computation.15 | convolution fusion | flops 11837374464 | bytes 38805504 | tf_op jit(solution)/shard_map/dot_general | solution.py:70
  301.7 20.6 %multiply_reduce_fusion = (f32[1024]{0:T(1024)S(1)}, f32[1024]{0:T(1024)S(1)}, f32[1024,1024]{0,1:T(8,128)}) fusion(f32[1024,1024]{0,1:T(8,128)} %get-tuple-element.204, f32[1024]{0:T(1024)S(1)} %fusion.136, f32[1024]{0:T(1024)S(1)} %reshape.802, bf16[1024,5632]{1,0:T(8,128)(2,1)} %all-gather.6.cloned.1.call-done, ...), kind=kOutput, calls=%fused_computation.47 | convolution fusion | flops 11840518144 | bytes 31473664 | tf_op jit(solution)/shard_map/dot_general | solution.py:76
  322.4 12.0 %fusion.66 = f32[2816,1024]{1,0:T(8,128)} fusion(bf16[1024,2816]{1,0:T(8,128)(2,1)} %get-tuple-element.147, bf16[1024,1024]{0,1:T(8,128)(2,1)S(1)} %copy-done.21, f32[1024]{0:T(1024)S(1)} %fusion.134), kind=kOutput, calls=%fused_computation.112 | convolution fusion | flops 5908725760 | bytes 19402752 | tf_op jit(solution)/shard_map/dot_general | solution.py:70
  334.4 4.7 fusion.142
  340.4 6.0 fusion.63
  346.4 5.6 reshape.781
  352.0 7.7 multiply_reduce_fusion.1
  361.5 9.3 fusion.172
  370.8 3.9 fusion.30
  374.9 4.4 fusion.147
  379.5 3.5 multiply_dynamic-update-slice_fusion
  396.4 11.8 %fusion.76 = (f32[16,4,128]{2,1,0:T(4,128)S(1)}, f32[16,4,128,64]{2,3,1,0:T(8,128)}) fusion(f32[16,64,4,128]{3,2,1,0:T(4,128)} %reshape.777, f32[16,4,128]{2,1,0:T(4,128)S(1)} %copy-done.41, f32[16,64,4,128]{3,0,1,2:T(8,128)S(1)} %copy-done.1, f32[16,4,128,256]{3,2,1,0:T(8,128)} %broadcast_dynamic-update-slice_fusion, f32[16,64,4,256]{3,2,1,0:T(4,128)} %reshape.771), kind=kOutput, calls=%fused_computation.118 | convolution fusion | flops 807395328 | bytes 18939904 | tf_op jit(solution)/shard_map/transpose(jvp(nshc,nshv->nhcv))/dot_general | solution.py:45
  408.3 9.5 fusion.82
  440.8 4.5 fusion.48
  445.3 3.2 multiply_negate_fusion
  452.4 4.4 fusion.173
  469.0 9.4 fusion.151
  478.5 6.7 fusion.6
  485.2 3.4 fusion.13
  489.8 11.5 %pad_maximum_fusion = f32[1024,4224]{1,0:T(8,128)} fusion(f32[1024,128]{1,0:T(8,128)S(1)} %reshape.791, f32[1024,1024]{1,0:T(8,128)} %fusion.173, f32[1024,3072]{1,0:T(8,128)} %fusion.151), kind=kLoop, calls=%fused_computation | loop fusion | flops 8650752 | bytes 34603008 | tf_op jit(solution)/shard_map/concatenate | solution.py:227
  502.5 12.2 %multiply_convert_fusion.2 = bf16[1024,1024]{0,1:T(8,128)(2,1)} fusion(f32[1024,1024]{0,1:T(8,128)} %get-tuple-element.204, f32[1024]{0:T(1024)S(1)} %fusion.134, bf16[1024,2816]{1,0:T(8,128)(2,1)} %get-tuple-element.147, bf16[2816,1024]{1,0:T(8,128)(2,1)} %all-gather.8.cloned.1.call-done), kind=kOutput, calls=%fused_computation.53 | convolution fusion | flops 5908725760 | bytes 17829888 | tf_op jit(solution)/shard_map/dot_general | solution.py:66
  514.7 4.1 copy.267
  518.8 8.9 fusion.20
  527.7 4.1 copy.268
  531.8 163.8 %reduce-scatter.4.cloned.1.call-done = f32[32,4224]{1,0:T(8,128)} async-done(((f32[1024,4224]{1,0:T(8,128)}), f32[32,4224]{1,0:T(8,128)}) %reduce-scatter.4.cloned.1.call-update) | async-done | bytes 540688 | tf_op jit(solution)/shard_map/reduce_scatter | solution.py:90
  703.0 240.0 %reduce-scatter.6.cloned.1.call-done = f32[32,5632]{1,0:T(8,128)} async-done(((f32[1024,5632]{1,0:T(8,128)}), f32[32,5632]{1,0:T(8,128)}) %reduce-scatter.6.cloned.1.call-update) | async-done | bytes 720912 | tf_op jit(solution)/shard_map/reduce_scatter | solution.py:90
  945.0 160.9 %reduce-scatter.8.cloned.1.call-done = f32[88,1024]{1,0:T(8,128)} async-done(((f32[2816,1024]{1,0:T(8,128)}), f32[88,1024]{1,0:T(8,128)}) %reduce-scatter.8.cloned.1.call-update) | async-done | bytes 360464 | tf_op jit(solution)/shard_map/reduce_scatter | solution.py:90
  (375 shorter events, 112.8 us)
Async XLA Ops:
  7.2 90.5 %all-gather.4.cloned.1.call-start = ((), (), s32[]{:S(2)}) async-start(), calls=%async_computation.3 | async-start | bytes 8921088 | tf_op jit(solution)/shard_map/all_gather | solution.py:86
  16.4 180.1 %all-gather.6.cloned.1.call-start = ((), (), s32[]{:S(2)}) async-start(), calls=%async_computation.4 | async-start | bytes 11894784 | tf_op jit(solution)/shard_map/all_gather | solution.py:86
  18.3 241.3 %all-gather.8.cloned.1.call-start = ((), (), s32[]{:S(2)}) async-start(), calls=%async_computation.5 | async-start | bytes 5947392 | tf_op jit(solution)/shard_map/all_gather | solution.py:86
  19.0 676.6 %reduce-scatter.4.cloned.1.call-start = ((), (), s32[]{:S(2)}) async-start(), calls=%async_computation.6 | async-start | bytes 17842176 | tf_op jit(solution)/shard_map/reduce_scatter | solution.py:90
  21.1 154.3 %copy-start.38 = (f32[64,64]{1,0:T(8,128)}, f32[64,64]{1,0:T(8,128)S(1)}, u32[]{:S(2)}) copy-start(f32[64,64]{1,0:T(8,128)S(1)} %fusion.132) | copy-start | bytes 49156
  27.1 88.3 %copy-start.15 = (bf16[1024,1024]{0,1:T(8,128)(2,1)}, bf16[1024,1024]{0,1:T(8,128)(2,1)S(1)}, u32[]{:S(2)}) copy-start(bf16[1024,1024]{0,1:T(8,128)(2,1)S(1)} %copy.208) | copy-start | bytes 6291460
  27.5 14.3 %copy-start.76 = (f32[1024]{0:T(1024)}, f32[1024]{0:T(1024)S(1)}, u32[]{:S(2)}) copy-start(f32[1024]{0:T(1024)S(1)} %fusion.21) | copy-start | bytes 12292
  27.6 87.8 %copy-start.84 = (f32[1024]{0:T(1024)}, f32[1024]{0:T(1024)S(1)}, u32[]{:S(2)}) copy-start(f32[1024]{0:T(1024)S(1)} %fusion.135) | copy-start | bytes 12292
  99.0 16.4 %copy-start.78 = (f32[1024]{0:T(1024)}, f32[1024]{0:T(1024)S(1)}, u32[]{:S(2)}) copy-start(f32[1024]{0:T(1024)S(1)} %reshape.799) | copy-start | bytes 12292
  122.7 47.4 %copy-start = (f32[16,64,4,128]{3,0,1,2:T(8,128)}, f32[16,64,4,128]{3,0,1,2:T(8,128)S(1)}, u32[]{:S(2)}) copy-start(f32[16,64,4,128]{3,0,1,2:T(8,128)S(1)} %fusion.55) | copy-start | bytes 6291460
  133.3 8.8 copy-start.40
  149.7 16.3 %copy-start.2 = (f32[16,4,128,256]{3,2,1,0:T(8,128)}, f32[16,4,128,256]{3,2,1,0:T(8,128)S(1)}, u32[]{:S(2)}) copy-start(f32[16,4,128,256]{3,2,1,0:T(8,128)S(1)} %fusion.32) | copy-start | bytes 25165828
  152.1 12.9 %copy-start.53 = (f32[1,1,4,128]{3,1,2,0:T(1,128)}, f32[1,1,4,128]{3,1,2,0:T(1,128)S(1)}, u32[]{:S(2)}) copy-start(f32[1,1,4,128]{3,1,2,0:T(1,128)S(1)} %get-tuple-element.159) | copy-start | bytes 6148
  152.1 12.9 %copy-start.70 = (f32[1,1,4,128]{3,1,2,0:T(1,128)}, f32[1,1,4,128]{3,1,2,0:T(1,128)S(1)}, u32[]{:S(2)}) copy-start(f32[1,1,4,128]{3,1,2,0:T(1,128)S(1)} %get-tuple-element.158) | copy-start | bytes 6148
  152.2 13.9 %copy-start.90 = (f32[1,1,4,128]{3,1,2,0:T(1,128)}, f32[1,1,4,128]{3,1,2,0:T(1,128)S(1)}, u32[]{:S(2)}) copy-start(f32[1,1,4,128]{3,1,2,0:T(1,128)S(1)} %get-tuple-element.157) | copy-start | bytes 6148
  152.2 41.9 %copy-start.45 = (f32[1,1,4,128]{3,1,2,0:T(1,128)}, f32[1,1,4,128]{3,1,2,0:T(1,128)S(1)}, u32[]{:S(2)}) copy-start(f32[1,1,4,128]{3,1,2,0:T(1,128)S(1)} %get-tuple-element.161) | copy-start | bytes 6148
  152.2 41.9 %copy-start.47 = (f32[1,1,4,128]{3,1,2,0:T(1,128)}, f32[1,1,4,128]{3,1,2,0:T(1,128)S(1)}, u32[]{:S(2)}) copy-start(f32[1,1,4,128]{3,1,2,0:T(1,128)S(1)} %get-tuple-element.165) | copy-start | bytes 6148
  152.2 41.9 %copy-start.49 = (f32[1,1,4,128]{3,1,2,0:T(1,128)}, f32[1,1,4,128]{3,1,2,0:T(1,128)S(1)}, u32[]{:S(2)}) copy-start(f32[1,1,4,128]{3,1,2,0:T(1,128)S(1)} %get-tuple-element.167) | copy-start | bytes 6148
  152.2 41.9 %copy-start.51 = (f32[1,1,4,128]{3,1,2,0:T(1,128)}, f32[1,1,4,128]{3,1,2,0:T(1,128)S(1)}, u32[]{:S(2)}) copy-start(f32[1,1,4,128]{3,1,2,0:T(1,128)S(1)} %get-tuple-element.169) | copy-start | bytes 6148
  152.2 41.9 %copy-start.55 = (f32[1,1,4,128]{3,1,2,0:T(1,128)}, f32[1,1,4,128]{3,1,2,0:T(1,128)S(1)}, u32[]{:S(2)}) copy-start(f32[1,1,4,128]{3,1,2,0:T(1,128)S(1)} %get-tuple-element.163) | copy-start | bytes 6148
  152.2 41.9 %copy-start.57 = (f32[1,1,4,128]{3,1,2,0:T(1,128)}, f32[1,1,4,128]{3,1,2,0:T(1,128)S(1)}, u32[]{:S(2)}) copy-start(f32[1,1,4,128]{3,1,2,0:T(1,128)S(1)} %get-tuple-element.164) | copy-start | bytes 6148
  152.2 41.9 %copy-start.59 = (f32[1,1,4,128]{3,1,2,0:T(1,128)}, f32[1,1,4,128]{3,1,2,0:T(1,128)S(1)}, u32[]{:S(2)}) copy-start(f32[1,1,4,128]{3,1,2,0:T(1,128)S(1)} %get-tuple-element.168) | copy-start | bytes 6148
  152.2 41.9 %copy-start.61 = (f32[1,1,4,128]{3,1,2,0:T(1,128)}, f32[1,1,4,128]{3,1,2,0:T(1,128)S(1)}, u32[]{:S(2)}) copy-start(f32[1,1,4,128]{3,1,2,0:T(1,128)S(1)} %get-tuple-element.166) | copy-start | bytes 6148
  152.2 41.9 %copy-start.63 = (f32[1,1,4,128]{3,1,2,0:T(1,128)}, f32[1,1,4,128]{3,1,2,0:T(1,128)S(1)}, u32[]{:S(2)}) copy-start(f32[1,1,4,128]{3,1,2,0:T(1,128)S(1)} %get-tuple-element.160) | copy-start | bytes 6148
  152.3 41.9 %copy-start.65 = (f32[1,1,4,128]{3,1,2,0:T(1,128)}, f32[1,1,4,128]{3,1,2,0:T(1,128)S(1)}, u32[]{:S(2)}) copy-start(f32[1,1,4,128]{3,1,2,0:T(1,128)S(1)} %get-tuple-element.162) | copy-start | bytes 6148
  152.3 41.9 %copy-start.72 = (f32[1,1,4,128]{3,1,2,0:T(1,128)}, f32[1,1,4,128]{3,1,2,0:T(1,128)S(1)}, u32[]{:S(2)}) copy-start(f32[1,1,4,128]{3,1,2,0:T(1,128)S(1)} %get-tuple-element.170) | copy-start | bytes 6148
  152.3 41.9 %copy-start.74 = (f32[1,1,4,128]{3,1,2,0:T(1,128)}, f32[1,1,4,128]{3,1,2,0:T(1,128)S(1)}, u32[]{:S(2)}) copy-start(f32[1,1,4,128]{3,1,2,0:T(1,128)S(1)} %get-tuple-element.171) | copy-start | bytes 6148
  187.0 147.5 %copy-start.80 = (f32[1024]{0:T(1024)}, f32[1024]{0:T(1024)S(1)}, u32[]{:S(2)}) copy-start(f32[1024]{0:T(1024)S(1)} %reshape.802) | copy-start | bytes 12292
  187.0 7.3 slice-start
  187.0 7.3 slice-start.1
  194.2 140.2 %copy-start.86 = (f32[1024]{0:T(1024)}, f32[1024]{0:T(1024)S(1)}, u32[]{:S(2)}) copy-start(f32[1024]{0:T(1024)S(1)} %fusion.136) | copy-start | bytes 12292
  196.5 63.1 %copy-start.21 = (bf16[1024,1024]{0,1:T(8,128)(2,1)S(1)}, bf16[1024,1024]{0,1:T(8,128)(2,1)}, u32[]{:S(2)}) copy-start(bf16[1024,1024]{0,1:T(8,128)(2,1)} %copy.241) | copy-start | bytes 6291460
  322.4 12.1 %copy-start.82 = (f32[1024]{0:T(1024)}, f32[1024]{0:T(1024)S(1)}, u32[]{:S(2)}) copy-start(f32[1024]{0:T(1024)S(1)} %multiply_multiply_fusion.2) | copy-start | bytes 12292
  352.0 7.8 copy-start.44
  352.0 7.8 copy-start.9
  361.5 9.4 copy-start.5
  379.3 15.4 %copy-start.3 = (f32[16,4,128,256]{3,2,1,0:T(8,128)}, f32[16,4,128,256]{3,2,1,0:T(8,128)S(1)}, u32[]{:S(2)}) copy-start(f32[16,4,128,256]{3,2,1,0:T(8,128)S(1)} %fusion.147) | copy-start | bytes 25165828
  392.9 24.9 %slice-start.2 = ((s8[8388608]{0:T(1024)(128)(4,1)}), s8[4194304]{0:T(1024)(128)(4,1)S(1)}, s32[]{:S(2)}) async-start(s8[8388608]{0:T(1024)(128)(4,1)} %bitcast.401), calls=%async_computation.11 | async-start | bytes 8388608
  396.4 21.3 %slice-start.3 = ((s8[8388608]{0:T(1024)(128)(4,1)}), s8[4194304]{0:T(1024)(128)(4,1)S(1)}, s32[]{:S(2)}) async-start(s8[8388608]{0:T(1024)(128)(4,1)} %bitcast.401), calls=%async_computation.12 | async-start | bytes 8388608
  408.3 9.5 copy-start.26
  408.3 9.5 copy-start.31
  427.5 13.2 %copy-start.12 = (f32[16,64,4,128]{3,2,1,0:T(4,128)S(1)}, f32[16,64,4,128]{3,2,1,0:T(4,128)}, u32[]{:S(2)}) copy-start(f32[16,64,4,128]{3,2,1,0:T(4,128)} %reshape.772) | copy-start | bytes 6291460
  427.5 13.2 %copy-start.25 = (f32[16,4,128,64]{2,3,1,0:T(8,128)S(1)}, f32[16,4,128,64]{2,3,1,0:T(8,128)}, u32[]{:S(2)}) copy-start(f32[16,4,128,64]{2,3,1,0:T(8,128)} %get-tuple-element.207) | copy-start | bytes 6291460
  468.6 9.8 slice-start.8
  469.0 9.5 slice-start.9
  469.0 9.5 slice-start.10
  501.3 441.7 %reduce-scatter.6.cloned.1.call-start = ((), (), s32[]{:S(2)}) async-start(), calls=%async_computation.7 | async-start | bytes 23789568 | tf_op jit(solution)/shard_map/reduce_scatter | solution.py:90
  501.9 604.0 %reduce-scatter.8.cloned.1.call-start = ((), (), s32[]{:S(2)}) async-start(), calls=%async_computation.8 | async-start | bytes 11894784 | tf_op jit(solution)/shard_map/reduce_scatter | solution.py:90
  (63 other events, 242.8 us)
Sparse Core Ops, SparseCore 0:
  16.5 81.1 all-gather.3
  101.2 89.7 all-gather.5
  193.8 65.7 all-gather.7
  501.4 194.1 reduce-scatter.3
  697.8 245.1 reduce-scatter.5
  945.7 160.1 reduce-scatter.7
